TPU v7x, 512 devices: a whole 4x4x16 slice. The times are simulated.
512 devices in a mesh: row: 32 (over x, y, core), col: 16 (over z).
Axes of the slice: x: 4, y: 4, z: 16, core: 2. Of those that a mesh axis runs over, the one named last changes fastest.
Arguments:
- spectra: bfloat16 [128, 2, 33, 4096], P('row', None, None, 'col'), may hold values from -64 to 64
- tilt_ranges: int32 [128, 2], P('row'), may hold values from 8 to 64
Outputs:
- correlation: float32 [128, 128, 729], P('row', 'col')
All inputs are finite; a program needn't handle non-finite values.
Results may differ from a plain program's by a relative error of at most 0.0003.
Values may be sent and summed in bfloat16 or wider, within the bound.
A program may use at most 128 MiB of HBM per device.

v0:
```python
import jax
import jax.numpy as jnp
from jax import lax
from jax.sharding import PartitionSpec as P

EDGE = 64
HALF = 33
REACH = 4
LAGS = 9
WINDOW = 729


full_turn = 2.0 * 3.141592653589793


def plane_table(offset, width):
    flat = offset + jnp.arange(width, dtype=jnp.int32)
    freq_x = flat // EDGE
    freq_y = flat % EDGE
    lag_x = jnp.repeat(jnp.arange(-REACH, REACH + 1, dtype=jnp.int32), LAGS)
    lag_y = jnp.tile(jnp.arange(-REACH, REACH + 1, dtype=jnp.int32), LAGS)
    phase = jnp.mod(freq_x[:, None] * lag_x[None, :] + freq_y[:, None] * lag_y[None, :], EDGE)
    angle = phase.astype(jnp.float32) * (full_turn / EDGE)
    cosine = jnp.cos(angle)
    sine = jnp.sin(angle)
    upper = jnp.concatenate([cosine, sine], 1)
    lower = jnp.concatenate([-sine, cosine], 1)
    return jnp.concatenate([upper, lower], 0)


def depth_table():
    freq_z = jnp.arange(HALF, dtype=jnp.int32)
    lag_z = jnp.arange(-REACH, REACH + 1, dtype=jnp.int32)
    phase = jnp.mod(freq_z[:, None] * lag_z[None, :], EDGE)
    angle = phase.astype(jnp.float32) * (full_turn / EDGE)
    return (jnp.cos(angle), jnp.sin(angle))


def depth_weights():
    freq_z = jnp.arange(HALF, dtype=jnp.int32)
    return jnp.where((freq_z == 0) | (freq_z == EDGE // 2), 1.0, 2.0).astype(jnp.float32)


def wedge_masks(tilt_ranges, offset, width):
    flat = offset + jnp.arange(width, dtype=jnp.int32)
    freq_x = flat // EDGE
    signed_x = jnp.where(freq_x < EDGE // 2, freq_x, freq_x - EDGE)
    freq_z = jnp.arange(HALF, dtype=jnp.int32)
    slopes = jnp.where(signed_x[None, :] > 0, tilt_ranges[:, 0:1], tilt_ranges[:, 1:2])
    observed = 16 * freq_z[None, :, None] <= slopes[:, None, :] * jnp.abs(signed_x)[None, None, :]
    return observed.astype(jnp.float32)


def pair_terms(own, own_mask, partner, partner_mask, table, depth_cos, depth_sin, weights):
    highest = lax.Precision.HIGHEST
    count_own = own.shape[0]
    count_partner = partner.shape[0]
    width = own.shape[3]
    own_real = own[:, 0].astype(jnp.float32)
    own_imag = own[:, 1].astype(jnp.float32)
    partner_real = partner[:, 0].astype(jnp.float32)
    partner_imag = partner[:, 1].astype(jnp.float32)
    joint = own_mask[:, None] * partner_mask[None, :] * weights[None, None, :, None]
    prod_real = (
        own_real[:, None] * partner_real[None] + own_imag[:, None] * partner_imag[None]
    ) * joint
    prod_imag = (
        own_imag[:, None] * partner_real[None] - own_real[:, None] * partner_imag[None]
    ) * joint
    mixed = jnp.dot(
        prod_real.reshape(-1, width),
        table[:width],
        precision=highest,
        preferred_element_type=jnp.float32,
    )
    mixed = mixed + jnp.dot(
        prod_imag.reshape(-1, width),
        table[width:],
        precision=highest,
        preferred_element_type=jnp.float32,
    )
    mixed = mixed.reshape(count_own, count_partner, HALF, 2 * LAGS * LAGS)
    plane_lags = LAGS * LAGS
    window = jnp.einsum("abzq,zl->abql", mixed[..., :plane_lags], depth_cos, precision=highest)
    window = window - jnp.einsum(
        "abzq,zl->abql", mixed[..., plane_lags:], depth_sin, precision=highest
    )
    window = window.reshape(count_own, count_partner, WINDOW)
    own_power = (own_real * own_real + own_imag * own_imag) * weights[None, :, None] * own_mask
    partner_power = (
        (partner_real * partner_real + partner_imag * partner_imag)
        * weights[None, :, None]
        * partner_mask
    )
    energy_own = jnp.einsum("azw,bzw->ab", own_power, partner_mask, precision=highest)
    energy_other = jnp.einsum("azw,bzw->ab", own_mask, partner_power, precision=highest)
    return (window, energy_own, energy_other)


def finish_sums(window, energy_own, energy_other):
    summed, total_own, total_other = (
        lax.psum_scatter(window, "col", scatter_dimension=1, tiled=True),
        lax.psum_scatter(energy_own, "col", scatter_dimension=1, tiled=True),
        lax.psum_scatter(energy_other, "col", scatter_dimension=1, tiled=True),
    )
    return summed / jnp.sqrt(total_own * total_other)[:, :, None]


def body(spectra, tilt_ranges):
    blocks = lax.axis_size("row")
    width = spectra.shape[3]
    block = spectra.shape[0]
    offset = lax.axis_index("col") * width
    table = plane_table(offset, width)
    depth_cos, depth_sin = depth_table()
    weights = depth_weights()
    own_mask = wedge_masks(tilt_ranges, offset, width)
    gathered, gathered_tilts = (
        lax.all_gather(spectra, "row", axis=0, tiled=True),
        lax.all_gather(tilt_ranges, "row", axis=0, tiled=True),
    )
    groups = blocks // 4
    group_size = 4 * block

    def one_group(inputs):
        portion, portion_tilts = inputs
        portion_mask = wedge_masks(portion_tilts, offset, width)
        return pair_terms(
            spectra, own_mask, portion, portion_mask, table, depth_cos, depth_sin, weights
        )

    grouped = gathered.reshape(groups, group_size, 2, HALF, width)
    grouped_tilts = gathered_tilts.reshape(groups, group_size, 2)
    window_groups, own_groups, other_groups = lax.map(one_group, (grouped, grouped_tilts))
    window = jnp.swapaxes(window_groups, 0, 1).reshape(block, groups * group_size, WINDOW)
    energy_own = jnp.swapaxes(own_groups, 0, 1).reshape(block, groups * group_size)
    energy_other = jnp.swapaxes(other_groups, 0, 1).reshape(block, groups * group_size)
    return finish_sums(window, energy_own, energy_other)


def solution(mesh):
    return jax.shard_map(
        body,
        mesh=mesh,
        in_specs=(P("row", None, None, "col"), P("row", None)),
        out_specs=P("row", "col", None),
        check_vma=False,
    )
```

profile of v0, /device:TPU:24, one launch (start us, length us, event | category | flops | bytes accessed | tf_op | source)
XLA Modules:
  0.0 507.9 jit_solution(8904417393397914571)
XLA Ops:
  9.2 26.7 %all-gather = s32[32,4,2]{1,2,0:T(2,128)S(1)} all-gather(s32[1,4,2]{1,2,0:T(2,128)} %bitcast.119), channel_id=1, replica_groups=mesh['row'=32,'col'=16] {'row'}, dimensions={0}, use_global_device_ids=true | all-gather | bytes 1056 | tf_op jit(solution)/shard_map/all_gather | solution.py:120
  38.5 37.6 %all-gather.3.cloned.1.call-done = bf16[128,2,33,256]{3,1,2,0:T(2,128)(2,1)} async-done(((bf16[4,2,33,256]{3,1,2,0:T(2,128)(2,1)}), bf16[128,2,33,256]{3,1,2,0:T(2,128)(2,1)}) %all-gather.3.cloned.1.call-update) | async-done | bytes 4325392 | tf_op jit(solution)/shard_map/all_gather | solution.py:119
  76.0 340.6 %while.19 = (s32[]{:T(128)}, f32[8,4,16,729]{2,1,3,0:T(4,128)}, f32[8,4,16]{2,1,0:T(4,128)S(1)}, f32[8,4,16]{2,1,0:T(4,128)S(1)}, bf16[4,2,33,256]{3,0,2,1:T(4,1...) while((s32[]{:T(128)}, f32[8,4,16,729]{2,1,3,0:T(4,128)}, ...), condition=%wide.region_1.2_spmd.clone.clone.clone, body=%wide.region_0.1_spmd.clone.clone.clone.sunk | while | flops 2160653824 | bytes 56682484 | solution.py:134
  87.5 3.9 multiply_subtract_fusion.2
  94.3 5.2 %fusion.110 = f32[2112,162]{0,1:T(8,128)} fusion(f32[256,162]{1,0:T(8,128)S(1)} %copy-done.1, f32[2112,256]{1,0:T(8,128)} %add.339, f32[2112,256]{1,0:T(8,128)S(1)} %mul.967, f32[2112]{0:T(1024)S(1)} %mul.969), kind=kOutput, calls=%fused_computation.8.clone.1 | convolution fusion | flops 1052147712 | bytes 5868288 | tf_op jit(solution)/shard_map/while/body/eval_jaxpr/dot_general | solution.py:70
  102.5 5.7 %convolution_add_fusion.2 = f32[2112,162]{0,1:T(8,128)} fusion(f32[2112,162]{0,1:T(8,128)} %fusion.110, f32[256,162]{1,0:T(8,128)S(1)} %copy-done, f32[2112,256]{1,0:T(8,128)} %sub.88, f32[2112,256]{1,0:T(8,128)S(1)} %mul.967, f32[2112]{0:T(1024)S(1)} %mul.969), kind=kOutput, calls=%fused_computation.4.clone.1 | convolution fusion | flops 1052489856 | bytes 7236864 | tf_op jit(solution)/shard_map/while/body/eval_jaxpr/dot_general | solution.py:76
  130.1 3.9 multiply_subtract_fusion.2
  136.9 5.2 %fusion.110 = f32[2112,162]{0,1:T(8,128)} fusion(f32[256,162]{1,0:T(8,128)S(1)} %copy-done.1, f32[2112,256]{1,0:T(8,128)} %add.339, f32[2112,256]{1,0:T(8,128)S(1)} %mul.967, f32[2112]{0:T(1024)S(1)} %mul.969), kind=kOutput, calls=%fused_computation.8.clone.1 | convolution fusion | flops 1052147712 | bytes 5868288 | tf_op jit(solution)/shard_map/while/body/eval_jaxpr/dot_general | solution.py:70
  145.1 5.7 %convolution_add_fusion.2 = f32[2112,162]{0,1:T(8,128)} fusion(f32[2112,162]{0,1:T(8,128)} %fusion.110, f32[256,162]{1,0:T(8,128)S(1)} %copy-done, f32[2112,256]{1,0:T(8,128)} %sub.88, f32[2112,256]{1,0:T(8,128)S(1)} %mul.967, f32[2112]{0:T(1024)S(1)} %mul.969), kind=kOutput, calls=%fused_computation.4.clone.1 | convolution fusion | flops 1052489856 | bytes 7236864 | tf_op jit(solution)/shard_map/while/body/eval_jaxpr/dot_general | solution.py:76
  179.5 5.2 %fusion.110 = f32[2112,162]{0,1:T(8,128)} fusion(f32[256,162]{1,0:T(8,128)S(1)} %copy-done.1, f32[2112,256]{1,0:T(8,128)} %add.339, f32[2112,256]{1,0:T(8,128)S(1)} %mul.967, f32[2112]{0:T(1024)S(1)} %mul.969), kind=kOutput, calls=%fused_computation.8.clone.1 | convolution fusion | flops 1052147712 | bytes 5868288 | tf_op jit(solution)/shard_map/while/body/eval_jaxpr/dot_general | solution.py:70
  187.7 5.7 %convolution_add_fusion.2 = f32[2112,162]{0,1:T(8,128)} fusion(f32[2112,162]{0,1:T(8,128)} %fusion.110, f32[256,162]{1,0:T(8,128)S(1)} %copy-done, f32[2112,256]{1,0:T(8,128)} %sub.88, f32[2112,256]{1,0:T(8,128)S(1)} %mul.967, f32[2112]{0:T(1024)S(1)} %mul.969), kind=kOutput, calls=%fused_computation.4.clone.1 | convolution fusion | flops 1052489856 | bytes 7236864 | tf_op jit(solution)/shard_map/while/body/eval_jaxpr/dot_general | solution.py:76
  222.0 5.3 %fusion.110 = f32[2112,162]{0,1:T(8,128)} fusion(f32[256,162]{1,0:T(8,128)S(1)} %copy-done.1, f32[2112,256]{1,0:T(8,128)} %add.339, f32[2112,256]{1,0:T(8,128)S(1)} %mul.967, f32[2112]{0:T(1024)S(1)} %mul.969), kind=kOutput, calls=%fused_computation.8.clone.1 | convolution fusion | flops 1052147712 | bytes 5868288 | tf_op jit(solution)/shard_map/while/body/eval_jaxpr/dot_general | solution.py:70
  230.2 5.7 %convolution_add_fusion.2 = f32[2112,162]{0,1:T(8,128)} fusion(f32[2112,162]{0,1:T(8,128)} %fusion.110, f32[256,162]{1,0:T(8,128)S(1)} %copy-done, f32[2112,256]{1,0:T(8,128)} %sub.88, f32[2112,256]{1,0:T(8,128)S(1)} %mul.967, f32[2112]{0:T(1024)S(1)} %mul.969), kind=kOutput, calls=%fused_computation.4.clone.1 | convolution fusion | flops 1052489856 | bytes 7236864 | tf_op jit(solution)/shard_map/while/body/eval_jaxpr/dot_general | solution.py:76
  264.6 5.2 %fusion.110 = f32[2112,162]{0,1:T(8,128)} fusion(f32[256,162]{1,0:T(8,128)S(1)} %copy-done.1, f32[2112,256]{1,0:T(8,128)} %add.339, f32[2112,256]{1,0:T(8,128)S(1)} %mul.967, f32[2112]{0:T(1024)S(1)} %mul.969), kind=kOutput, calls=%fused_computation.8.clone.1 | convolution fusion | flops 1052147712 | bytes 5868288 | tf_op jit(solution)/shard_map/while/body/eval_jaxpr/dot_general | solution.py:70
  272.8 5.7 %convolution_add_fusion.2 = f32[2112,162]{0,1:T(8,128)} fusion(f32[2112,162]{0,1:T(8,128)} %fusion.110, f32[256,162]{1,0:T(8,128)S(1)} %copy-done, f32[2112,256]{1,0:T(8,128)} %sub.88, f32[2112,256]{1,0:T(8,128)S(1)} %mul.967, f32[2112]{0:T(1024)S(1)} %mul.969), kind=kOutput, calls=%fused_computation.4.clone.1 | convolution fusion | flops 1052489856 | bytes 7236864 | tf_op jit(solution)/shard_map/while/body/eval_jaxpr/dot_general | solution.py:76
  307.2 5.2 %fusion.110 = f32[2112,162]{0,1:T(8,128)} fusion(f32[256,162]{1,0:T(8,128)S(1)} %copy-done.1, f32[2112,256]{1,0:T(8,128)} %add.339, f32[2112,256]{1,0:T(8,128)S(1)} %mul.967, f32[2112]{0:T(1024)S(1)} %mul.969), kind=kOutput, calls=%fused_computation.8.clone.1 | convolution fusion | flops 1052147712 | bytes 5868288 | tf_op jit(solution)/shard_map/while/body/eval_jaxpr/dot_general | solution.py:70
  315.4 5.7 %convolution_add_fusion.2 = f32[2112,162]{0,1:T(8,128)} fusion(f32[2112,162]{0,1:T(8,128)} %fusion.110, f32[256,162]{1,0:T(8,128)S(1)} %copy-done, f32[2112,256]{1,0:T(8,128)} %sub.88, f32[2112,256]{1,0:T(8,128)S(1)} %mul.967, f32[2112]{0:T(1024)S(1)} %mul.969), kind=kOutput, calls=%fused_computation.4.clone.1 | convolution fusion | flops 1052489856 | bytes 7236864 | tf_op jit(solution)/shard_map/while/body/eval_jaxpr/dot_general | solution.py:76
  349.9 5.3 %fusion.110 = f32[2112,162]{0,1:T(8,128)} fusion(f32[256,162]{1,0:T(8,128)S(1)} %copy-done.1, f32[2112,256]{1,0:T(8,128)} %add.339, f32[2112,256]{1,0:T(8,128)S(1)} %mul.967, f32[2112]{0:T(1024)S(1)} %mul.969), kind=kOutput, calls=%fused_computation.8.clone.1 | convolution fusion | flops 1052147712 | bytes 5868288 | tf_op jit(solution)/shard_map/while/body/eval_jaxpr/dot_general | solution.py:70
  358.1 5.7 %convolution_add_fusion.2 = f32[2112,162]{0,1:T(8,128)} fusion(f32[2112,162]{0,1:T(8,128)} %fusion.110, f32[256,162]{1,0:T(8,128)S(1)} %copy-done, f32[2112,256]{1,0:T(8,128)} %sub.88, f32[2112,256]{1,0:T(8,128)S(1)} %mul.967, f32[2112]{0:T(1024)S(1)} %mul.969), kind=kOutput, calls=%fused_computation.4.clone.1 | convolution fusion | flops 1052489856 | bytes 7236864 | tf_op jit(solution)/shard_map/while/body/eval_jaxpr/dot_general | solution.py:76
  392.4 5.2 %fusion.110 = f32[2112,162]{0,1:T(8,128)} fusion(f32[256,162]{1,0:T(8,128)S(1)} %copy-done.1, f32[2112,256]{1,0:T(8,128)} %add.339, f32[2112,256]{1,0:T(8,128)S(1)} %mul.967, f32[2112]{0:T(1024)S(1)} %mul.969), kind=kOutput, calls=%fused_computation.8.clone.1 | convolution fusion | flops 1052147712 | bytes 5868288 | tf_op jit(solution)/shard_map/while/body/eval_jaxpr/dot_general | solution.py:70
  400.6 5.7 %convolution_add_fusion.2 = f32[2112,162]{0,1:T(8,128)} fusion(f32[2112,162]{0,1:T(8,128)} %fusion.110, f32[256,162]{1,0:T(8,128)S(1)} %copy-done, f32[2112,256]{1,0:T(8,128)} %sub.88, f32[2112,256]{1,0:T(8,128)S(1)} %mul.967, f32[2112]{0:T(1024)S(1)} %mul.969), kind=kOutput, calls=%fused_computation.4.clone.1 | convolution fusion | flops 1052489856 | bytes 7236864 | tf_op jit(solution)/shard_map/while/body/eval_jaxpr/dot_general | solution.py:76
  416.7 11.0 %copy.42 = f32[4,8,16,729]{3,2,1,0:T(8,128)} copy(f32[4,8,16,729]{2,0,3,1:T(4,128)} %bitcast.113) | data formatting | bytes 2985984 | tf_op jit(solution)/shard_map/transpose | solution.py:135
  429.8 31.3 %all-reduce.2 = (f32[4,128]{1,0:T(4,128)S(1)}, f32[4,128]{1,0:T(4,128)S(1)}) all-reduce(f32[4,128]{1,0:T(4,128)S(1)} %reshape.363, f32[4,128]{1,0:T(4,128)S(1)} %reshape.362), channel_id=4, replica_groups=mesh['row'=32,'col'=16] {'col'}, use_global_device_ids=true, to_apply=%region_4.5.clone | all-reduce | flops 1024 | bytes 8192
  461.2 38.2 %reduce-scatter.4.cloned.1.call-done = f32[4,8,729]{2,1,0:T(8,128)} async-done(((f32[4,128,729]{2,1,0:T(8,128)}), f32[4,8,729]{2,1,0:T(8,128)}) %reduce-scatter.4.cloned.1.call-update) | async-done | bytes 93328 | tf_op jit(solution)/shard_map/reduce_scatter | solution.py:102
  (332 shorter events, 252.8 us)
Async XLA Ops:
  6.5 69.5 %all-gather.3.cloned.1.call-start = ((), (), s32[]{:S(2)}) async-start(), calls=%async_computation.1 | async-start | bytes 4460544 | tf_op jit(solution)/shard_map/all_gather | solution.py:119
  7.3 492.2 %reduce-scatter.4.cloned.1.call-start = ((), (), s32[]{:S(2)}) async-start(), calls=%async_computation.2 | async-start | bytes 1671168 | tf_op jit(solution)/shard_map/reduce_scatter | solution.py:102
  91.4 2.9 copy-start.1
  99.6 2.9 copy-start
  134.0 2.9 copy-start.1
  142.1 2.9 copy-start
  176.6 2.9 copy-start.1
  184.7 2.9 copy-start
  219.1 2.9 copy-start.1
  227.3 2.9 copy-start
  261.7 2.9 copy-start.1
  269.9 2.9 copy-start
  304.3 2.9 copy-start.1
  312.5 2.9 copy-start
  346.9 2.9 copy-start.1
  355.1 2.9 copy-start
  389.5 2.9 copy-start.1
  397.7 2.9 copy-start
Sparse Core Ops, SparseCore 0:
  10.6 65.4 all-gather.2
  427.8 71.5 reduce-scatter.3
where the time goes:
time: 512 us; the launch traced here: 508 us
  local copies, waits for them, and re-layouts  176 us (34%)
  matrix products  122 us (24%)
  waiting for transfers between devices  76.5 us (15%)
  other arithmetic  59.6 us (12%)
  blocking collectives  58 us (11%)
  between operations  14.1 us (3%)
    dot_general x8, matrix products, pair_terms(): jnp.dot(prod_imag.reshape(-1, width), table[width:], precision=highest, p...  45.2 us
    dot_general x8, matrix products, pair_terms(): jnp.dot(prod_real.reshape(-1, width), table[:width], precision=highest, p...  42 us
    reduce_scatter x1, waiting for transfers between devices, finish_sums(): lax.psum_scatter(window, 'col', scatter_dimension=1, tiled=True)  38.2 us
    all_gather x1, waiting for transfers between devices, body(): lax.all_gather(spectra, 'row', axis=0, tiled=True)  37.6 us
    unnamed x1, blocking collectives  31.3 us
    sub x8, other arithmetic, pair_terms(): own_imag[:, None] * partner_real[None]  31.3 us
    all_gather x1, blocking collectives, body(): lax.all_gather(tilt_ranges, 'row', axis=0, tiled=True)  26.7 us
    sub x8, local copies, waits for them, and re-layouts, pair_terms(): own_imag[:, None] * partner_real[None]  23.5 us
  transfers between devices with their start and end apart: 2, of which 2 were waited for; matrix products, arithmetic and copies ran while one was open for 1% of the time, Pallas kernels for 0%

commit v1 on v0

v1 whole, which is shorter than its diff:
```python
import functools
import math

import jax
import jax.numpy as jnp
import ml_dtypes
import numpy as np
from jax import lax
from jax.experimental import pallas as pl
from jax.experimental.pallas import tpu as pltpu
from jax.sharding import PartitionSpec as P

EDGE = 64
HALF = 33
REACH = 4
LAGS = 9
WINDOW = 729
PADDED = 768
TILES = HALF + 2
PIECE = 40
NT = (((1,), (1,)), ((), ()))


def split_np(x):
    high = x.astype(ml_dtypes.bfloat16)
    low = (x - high.astype(np.float64)).astype(ml_dtypes.bfloat16)
    return high, low


def y_table():
    freq = np.arange(EDGE)
    out = np.zeros((LAGS, 8, 128), np.float32)
    for i in range(LAGS):
        if i <= REACH:
            t = np.cos(2 * np.pi * freq * i / EDGE)
        else:
            t = np.sin(2 * np.pi * freq * (i - REACH) / EDGE)
        out[i, :, :EDGE] = t
        out[i, :4, EDGE:] = t
        out[i, 4:, EDGE:] = -t
    return out


def x_table(cols):
    out = np.zeros((cols, LAGS, 32, 2, 8, 4, 4), np.float64)
    for col in range(cols):
        for k in range(4):
            for lx in range(-REACH, REACH + 1):
                angle = 2 * np.pi * ((col * 4 + k) * lx % EDGE) / EDGE
                for r in range(8):
                    for s in range(4):
                        out[col, lx + REACH, r * 4 + s, 0, r, k, s] = math.cos(angle)
                        out[col, lx + REACH, r * 4 + s, 1, r, k, s] = -math.sin(angle)
    out = out.reshape(cols, LAGS * 32, 256)
    high, low = split_np(out)
    return np.concatenate([high, low], 1)


def z_coefs():
    weight = [1.0 if k in (0, 32) else 2.0 for k in range(HALF)]
    cos = [[weight[k] * math.cos(2 * math.pi * k * l / EDGE) for k in range(HALF)] for l in range(REACH + 1)]
    sin = [[weight[k] * math.sin(2 * math.pi * k * l / EDGE) for k in range(HALF)] for l in range(REACH + 1)]
    return cos, sin


def signed(freq_x):
    return jnp.where(freq_x < EDGE // 2, freq_x, freq_x - EDGE)


def observed(freq_z, freq_x, up, down):
    q = signed(freq_x)
    return 16 * freq_z <= jnp.where(q > 0, up, down) * jnp.abs(q)


def prepare(col, spectra, tilts, message, power, pieces):
    lanes = lax.broadcasted_iota(jnp.int32, (HALF, 256), 1)
    freq_z = lax.broadcasted_iota(jnp.int32, (HALF, 256), 0)
    freq_x = col * 4 + lanes // EDGE
    weight = jnp.where((freq_z == 0) | (freq_z == EDGE // 2), 1.0, 2.0).astype(jnp.float32)
    power[...] = jnp.zeros_like(power)
    row = lax.broadcasted_iota(jnp.int32, (16, 256), 0)
    lane = lax.broadcasted_iota(jnp.int32, (16, 256), 1)
    total = jnp.zeros((16, 128), jnp.float32)
    for s in range(4):
        mask = observed(freq_z, freq_x, tilts[s, 0], tilts[s, 1])
        real = jnp.where(mask, spectra[s, 0].astype(jnp.float32), 0.0)
        imag = jnp.where(mask, spectra[s, 1].astype(jnp.float32), 0.0)
        square = (real * real + imag * imag) * weight
        for p in range(3):
            power[PIECE * p : PIECE * p + HALF, :] = square
        chosen = jnp.where((row // 4 == lane // EDGE) & (row % 4 == s), 1.0, 0.0)
        total = total + lax.dot_general(
            chosen, power[...], NT, precision=lax.Precision.HIGHEST, preferred_element_type=jnp.float32
        )
        for k in range(4):
            part = slice(k * EDGE, (k + 1) * EDGE)
            pieces[:, k * 4 + s, :] = jnp.concatenate([real[:, part], imag[:, part]], axis=1)
    message[:HALF] = pieces[...].astype(jnp.bfloat16)
    lane = lax.broadcasted_iota(jnp.int32, (16, 128), 1)
    row = lax.broadcasted_iota(jnp.int32, (16, 128), 0)
    high = total.astype(jnp.bfloat16).astype(jnp.float32)
    rest = total - high
    mid = rest.astype(jnp.bfloat16).astype(jnp.float32)
    low = rest - mid
    third = lane // PIECE
    message[HALF] = jnp.where(third == 0, high, jnp.where(third == 1, mid, low)).astype(jnp.bfloat16)
    s = row % 4
    up, down = (
        jnp.where(s == 0, tilts[0, i], jnp.where(s == 1, tilts[1, i], jnp.where(s == 2, tilts[2, i], tilts[3, i])))
        for i in range(2)
    )
    at = lane - third * PIECE
    mask = observed(at, col * 4 + row // 4, up, down) & (at < HALF) & (third < 3)
    message[HALF + 1] = jnp.where(mask, 1.0, 0.0).astype(jnp.bfloat16)


def modulate(block, table, mod):
    def one(z, carry):
        base = block[z].astype(jnp.float32)
        turned = pltpu.roll(base, EDGE, 1)
        highs, lows = [], []
        for k in range(4):
            both = jnp.concatenate([base[4 * k : 4 * k + 4], turned[4 * k : 4 * k + 4]], axis=0)
            for i in range(LAGS):
                value = both * table[i]
                high = value.astype(jnp.bfloat16)
                highs.append(high)
                lows.append((value - high.astype(jnp.float32)).astype(jnp.bfloat16))
        mod[z, :, :128] = jnp.concatenate(highs, axis=0)
        mod[z, :, 128:] = jnp.concatenate(lows, axis=0)
        return carry

    lax.fori_loop(0, HALF, one, 0, unroll=3)


def window_tile(own, mod, blocks, depth, quads):
    lane_k = (lax.broadcasted_iota(jnp.int32, (8, 128), 1) // 4) % 4

    def diagonal(values):
        lane = jnp.concatenate([lane_k] * (values[0].shape[0] // 8), axis=0) if values[0].shape[0] > 8 else lane_k
        out = values[3]
        for k in (2, 1, 0):
            out = jnp.where(lane == k, values[k], out)
        return out

    def one(z, carry):
        tile = blocks(z)
        product = lax.dot_general(
            mod[z], jnp.concatenate([tile, tile], axis=1), NT, preferred_element_type=jnp.float32
        )
        depth[z] = diagonal([product[72 * k : 72 * k + 72] for k in range(4)]).reshape(LAGS, 8, 128)
        return carry

    lax.fori_loop(0, HALF, one, 0, unroll=11)

    energies = []
    for own_tile, other in ((HALF, HALF + 1), (HALF + 1, HALF)):
        product = lax.dot_general(own[own_tile], blocks(other), NT, preferred_element_type=jnp.float32)
        picked = jnp.zeros((4, 128), jnp.float32)
        for k in range(4):
            picked = jnp.where(lane_k[:4] == k, product[4 * k : 4 * k + 4], picked)
        energies.append(jnp.concatenate([picked, jnp.zeros((4, 128), jnp.float32)], axis=0))

    cos, sin = z_coefs()

    def along_z(i, carry):
        value = [depth[z, i] for z in range(HALF)]
        even = [value[z] + value[32 - z] for z in range(16)] + [value[16]]
        odd = [value[z] - value[32 - z] for z in range(16)] + [value[16]]
        for lag in range(REACH + 1):
            source = even if lag % 2 == 0 else odd
            total = None
            for z in range(17):
                c = cos[lag][z]
                if z == 16 and lag % 2 == 1 or abs(c) < 1e-12:
                    continue
                term = source[z] * c
                total = term if total is None else total + term
            quads[lag, i] = total
        for lag in range(1, REACH + 1):
            source = odd if lag % 2 == 0 else even
            total = None
            for z in range(17):
                c = sin[lag][z]
                if z == 16 and lag % 2 == 0 or abs(c) < 1e-12:
                    continue
                term = source[z] * c
                total = term if total is None else total + term
            quads[REACH + lag, i] = total
        return carry

    lax.fori_loop(0, LAGS, along_z, 0)

    half = lax.broadcasted_iota(jnp.int32, (8, 128), 0) < 4

    def times_i(x):
        y = pltpu.roll(x, 4, 0)
        return jnp.where(half, -y, y)

    q = {}
    for ly in range(REACH + 1):
        for lz in range(REACH + 1):
            cc = quads[lz, ly]
            if ly == 0 and lz == 0:
                q[0, 0] = cc
            elif ly == 0:
                g = times_i(quads[REACH + lz, 0])
                q[0, lz], q[0, -lz] = cc + g, cc - g
            elif lz == 0:
                g = times_i(quads[0, REACH + ly])
                q[ly, 0], q[-ly, 0] = cc + g, cc - g
            else:
                ss = quads[REACH + lz, REACH + ly]
                sc = quads[lz, REACH + ly]
                cs = quads[REACH + lz, ly]
                p, m = cc - ss, cc + ss
                g, h = times_i(sc + cs), times_i(sc - cs)
                q[ly, lz], q[-ly, -lz] = p + g, p - g
                q[ly, -lz], q[-ly, lz] = m + h, m - h
    order = [q[ly, lz] for ly in range(-REACH, REACH + 1) for lz in range(-REACH, REACH + 1)] + energies
    order = order + [jnp.zeros((8, 128), jnp.float32)] * 5
    return order


def window_out(order_ref, xt, s):
    real = order_ref[pl.ds(s, 88, stride=8), :]
    imag = order_ref[pl.ds(4 + s, 88, stride=8), :]
    value = jnp.concatenate([real, imag], axis=1)
    high = value.astype(jnp.bfloat16)
    low = (value - high.astype(jnp.float32)).astype(jnp.bfloat16)
    x_high, x_low = xt[:288], xt[288:]
    dot = functools.partial(lax.dot_general, dimension_numbers=NT, preferred_element_type=jnp.float32)
    out = dot(x_high, high) + (dot(x_low, high) + dot(x_high, low))
    pieces = [out[32 * i : 32 * i + 32, :81] for i in range(LAGS)]
    energy = out[32 * REACH : 32 * REACH + 32, 81:83]
    fill = jnp.zeros((32, PADDED - WINDOW - 2), jnp.float32)
    return jnp.concatenate(pieces + [energy, fill], axis=1)


def flip_rows(rows):
    moved = pltpu.roll(rows, PADDED - WINDOW, 1)
    stacked = jnp.concatenate([moved[:, 128 * (5 - i) : 128 * (6 - i)] for i in range(6)], axis=0)
    row = lax.broadcasted_iota(jnp.int32, (128, 128), 0)
    lane = lax.broadcasted_iota(jnp.int32, (128, 128), 1)
    swap = jnp.where(row + lane == 127, 1.0, 0.0).astype(jnp.bfloat16)
    out = None
    for _ in range(3):
        high = stacked.astype(jnp.bfloat16)
        stacked = stacked - high.astype(jnp.float32)
        part = jnp.dot(high, swap, preferred_element_type=jnp.float32)
        out = part if out is None else out + part
    return out


def fused_kernel(
    spectra_any, tilts_any, table_any, tables_any, out,
    spectra, tilts, table, xt, power, pieces, own, mods, lanes, mod, depth, quads, order,
    part, extra, from_left, from_right, extra_in, sent, final, turned,
    local_sem, x_send, x_recv, y_send, y_recv, right_send, right_recv, left_send, left_recv,
    extra_send, extra_recv, final_send, final_recv,
):
    row = lax.axis_index("row")
    z = lax.axis_index("col")
    xx, yy, core = row // 8, (row // 2) % 4, row % 2
    zx, zy = z // 4, z % 4
    chip = xx * 4 + yy

    def at(x, y, c, depth_z):
        return {"row": (x * 4 + y) * 2 + c, "col": depth_z}

    locals_ = [
        pltpu.make_async_copy(spectra_any, spectra, local_sem.at[0]),
        pltpu.make_async_copy(tilts_any, tilts, local_sem.at[1]),
        pltpu.make_async_copy(table_any, table, local_sem.at[2]),
        pltpu.make_async_copy(tables_any.at[z], xt, local_sem.at[3]),
    ]
    for copy in locals_:
        copy.start()

    barrier = pltpu.get_barrier_semaphore()

    def greet(target):
        pl.semaphore_signal(barrier, inc=1, device_id=target, device_id_type=pl.DeviceIdType.MESH)

    for i in range(1, 4):
        greet(at(lax.rem(xx + i, 4), yy, core, z))
        greet(at(xx, lax.rem(yy + i, 4), 0, z))
        greet(at(xx, lax.rem(yy + i, 4), 1, z))
    greet(at(xx, yy, 1 - core, z))
    right, left = lax.rem(z + 1, 16), lax.rem(z + 15, 16)
    greet(at(xx, yy, core, right))
    greet(at(xx, yy, core, left))

    @pl.when(zx != xx)
    def _():
        greet(at(zx, yy, core, xx * 4 + zy))

    @pl.when(zy != yy)
    def _():
        greet(at(xx, zy, 0, zx * 4 + yy))
        greet(at(xx, zy, 1, zx * 4 + yy))

    locals_[0].wait()
    locals_[1].wait()
    prepare(z, spectra, tilts, own, power, pieces)
    count = 12 + jnp.where(zx != xx, 1, 0) + jnp.where(zy != yy, 2, 0)
    pl.semaphore_wait(barrier, count)

    def remote(src, dst, send, recv, target):
        return pltpu.make_async_remote_copy(
            src_ref=src, dst_ref=dst, send_sem=send, recv_sem=recv,
            device_id=target, device_id_type=pl.DeviceIdType.MESH,
        )

    gathers = []
    for i in range(1, 4):
        y = lax.rem(yy + i, 4)
        there = jnp.where(y < yy, core, 1 - core)
        gathers.append(remote(own, lanes.at[yy], y_send.at[i], y_recv.at[yy], at(xx, y, there, z)))
    gathers.append(remote(own, lanes.at[4], y_send.at[0], y_recv.at[4], at(xx, yy, 1 - core, z)))
    for i in range(1, 4):
        x = lax.rem(xx + i, 4)
        gathers.append(remote(own, mods.at[xx], x_send.at[i], x_recv.at[xx], at(x, yy, core, z)))
    for copy in gathers:
        copy.start()

    lanes[yy] = own[...]
    mods[xx] = own[...]
    lanes[5:8] = jnp.zeros((3, TILES, 16, 128), jnp.bfloat16)
    locals_[2].wait()
    modulate(own, table, mod.at[0])
    locals_[3].wait()

    def wait_lane(slot):
        remote(own, lanes.at[slot], y_send.at[0], y_recv.at[slot], at(xx, yy, 1 - core, z)).wait_recv()

    for i in range(1, 4):
        wait_lane(lax.rem(yy + i, 4))
    wait_lane(4)

    def move_right(step):
        chunk = lax.rem(z + 9 - step, 16)
        if step > 1:
            before = remote(part.at[chunk], from_left.at[step - 2], right_send.at[step - 2], right_recv.at[step - 2], at(xx, yy, core, right))
            before.wait_recv()
            part[chunk] = part[chunk] + from_left[step - 2]
        remote(part.at[chunk], from_left.at[step - 1], right_send.at[step - 1], right_recv.at[step - 1], at(xx, yy, core, right)).start()

        @pl.when(chunk == chip)
        def _():
            copy = remote(extra, extra_in.at[0], extra_send.at[0], extra_recv.at[0], at(xx, yy, core, right))
            if step > 1:
                copy.wait_recv()
                extra[...] = extra[...] + extra_in[0]
            copy.start()

    def move_left(step):
        chunk = lax.rem(z + 8 + step, 16)
        if step > 1:
            before = remote(part.at[chunk], from_right.at[step - 2], left_send.at[step - 2], left_recv.at[step - 2], at(xx, yy, core, left))
            before.wait_recv()
            part[chunk] = part[chunk] + from_right[step - 2]
        remote(part.at[chunk], from_right.at[step - 1], left_send.at[step - 1], left_recv.at[step - 1], at(xx, yy, core, left)).start()

        @pl.when(chunk == chip)
        def _():
            copy = remote(extra, extra_in.at[1], extra_send.at[0], extra_recv.at[1], at(xx, yy, core, left))
            if step > 1:
                copy.wait_recv()
                extra[...] = extra[...] + extra_in[1]
            copy.start()

    second = jnp.where(zy < 2, 1, 3)

    def task(q, carry):
        turn = jnp.where(q == 0, 2, jnp.where(q == 1, second, jnp.where(q == 2, 4 - second, 0)))
        x = lax.rem(zx + turn, 4)

        @pl.when(x != xx)
        def _():
            remote(own, mods.at[x], x_send.at[0], x_recv.at[x], at(xx, yy, 1 - core, z)).wait_recv()
            modulate(mods.at[x], table, mod.at[1])

        def blocks(k):
            return lanes[:, k].reshape(128, 128)

        rows = window_tile(mods.at[x], mod.at[jnp.where(x == xx, 0, 1)], blocks, depth, quads)
        order[...] = jnp.concatenate(rows, axis=0)
        for s in range(4):
            value = window_out(order, xt, s)
            other = value[16:20]
            for y in range(4):
                swap = (yy == y) & (x < xx)
                part[x * 4 + y, 4 * s : 4 * s + 4, :] = jnp.where(swap, other, value[4 * y : 4 * y + 4])

            @pl.when(x == xx)
            def _():
                extra[4 * s : 4 * s + 4, :] = other

        @pl.when(q == 0)
        def _():
            move_right(1)

        @pl.when(q == 1)
        def _():
            for step in (2, 3):
                move_right(step)
                move_left(step - 1)

        @pl.when(q == 2)
        def _():
            for step in (4, 5):
                move_right(step)
                move_left(step - 1)

        return carry

    lax.fori_loop(0, 4, task, 0)
    for step in (6, 7, 8):
        move_right(step)
        move_left(step - 1)
    remote(part.at[z], from_left.at[7], right_send.at[7], right_recv.at[7], at(xx, yy, core, right)).wait_recv()
    remote(part.at[z], from_right.at[6], left_send.at[6], left_recv.at[6], at(xx, yy, core, left)).wait_recv()

    def scaled(total):
        return total / jnp.sqrt(total[:, WINDOW : WINDOW + 1] * total[:, WINDOW + 1 : WINDOW + 2])

    value = scaled(part[z] + from_left[7] + from_right[6])
    same_x = zx == xx
    home = z == chip
    keep = (zy == yy) & (zx >= xx)
    to_direct = remote(sent.at[0], final.at[0], final_send.at[0], final_recv.at[0], at(zx, yy, core, xx * 4 + zy))
    partner = jnp.where(zy != yy, jnp.where(yy < zy, core, 1 - core), 1 - core)
    to_turned = remote(sent.at[1], final.at[1], final_send.at[1], final_recv.at[1], at(xx, zy, partner, zx * 4 + yy))

    @pl.when(same_x)
    def _():
        final[0] = value

    @pl.when(jnp.logical_not(same_x))
    def _():
        sent[0] = value
        to_direct.start()

    turned[...] = flip_rows(value)
    flipped = jnp.concatenate(
        [
            jnp.concatenate([turned[pl.ds(16 * i + s, 4, stride=4), :] for i in range(6)], axis=1)
            for s in range(4)
        ],
        axis=0,
    )

    @pl.when(keep & jnp.logical_not(home))
    def _():
        final[1] = flipped

    @pl.when(jnp.logical_not(keep))
    def _():
        sent[1] = flipped
        to_turned.start()

    @pl.when(home)
    def _():
        for i, send in ((0, right), (1, left)):
            remote(extra, extra_in.at[i], extra_send.at[0], extra_recv.at[i], at(xx, yy, core, send)).wait_recv()
        final[1] = scaled(extra[...] + extra_in[0] + extra_in[1])

    @pl.when(jnp.logical_not(same_x))
    def _():
        to_direct.wait_recv()

    @pl.when(jnp.logical_not(keep))
    def _():
        to_turned.wait_recv()

    first = jnp.where(
        zy != yy,
        jnp.where(yy < zy, core, 1 - core),
        jnp.where(zx <= xx, core, 1 - core),
    )
    one, two = final[0], final[1]
    low = jnp.where(first == 0, one, two)
    high = jnp.where(first == 0, two, one)
    for a in range(4):
        out[a] = jnp.concatenate([low[4 * a : 4 * a + 4, :WINDOW], high[4 * a : 4 * a + 4, :WINDOW]], axis=0)

    @pl.when(jnp.logical_not(same_x))
    def _():
        to_direct.wait_send()

    @pl.when(jnp.logical_not(keep))
    def _():
        to_turned.wait_send()

    for copy in gathers:
        copy.wait_send()
    for i in range(8):
        remote(part.at[i], from_left.at[i], right_send.at[i], right_recv.at[i], at(xx, yy, core, right)).wait_send()
    for i in range(7):
        remote(part.at[i], from_right.at[i], left_send.at[i], left_recv.at[i], at(xx, yy, core, left)).wait_send()

    @pl.when(jnp.logical_not(home))
    def _():
        remote(extra, extra_in.at[0], extra_send.at[0], extra_recv.at[0], at(xx, yy, core, right)).wait_send()


def body(x_tables, table, spectra, tilt_ranges):
    anywhere = pl.BlockSpec(memory_space=pl.ANY)
    f32, bf16 = jnp.float32, jnp.bfloat16
    dma = pltpu.SemaphoreType.DMA
    return pl.pallas_call(
        fused_kernel,
        out_shape=jax.ShapeDtypeStruct((4, 8, WINDOW), f32),
        in_specs=[anywhere] * 4,
        out_specs=pl.BlockSpec(memory_space=pltpu.VMEM),
        scratch_shapes=[
            pltpu.VMEM((4, 2, HALF, 256), bf16),
            pltpu.SMEM((4, 2), jnp.int32),
            pltpu.VMEM((LAGS, 8, 128), f32),
            pltpu.VMEM((576, 256), bf16),
            pltpu.VMEM((128, 256), f32),
            pltpu.VMEM((HALF, 16, 128), f32),
            pltpu.VMEM((TILES, 16, 128), bf16),
            pltpu.VMEM((4, TILES, 16, 128), bf16),
            pltpu.VMEM((8, TILES, 16, 128), bf16),
            pltpu.VMEM((2, HALF, 288, 256), bf16),
            pltpu.VMEM((HALF, LAGS, 8, 128), f32),
            pltpu.VMEM((LAGS, LAGS, 8, 128), f32),
            pltpu.VMEM((88 * 8, 128), f32),
            pltpu.VMEM((16, 16, PADDED), f32),
            pltpu.VMEM((16, PADDED), f32),
            pltpu.VMEM((8, 16, PADDED), f32),
            pltpu.VMEM((7, 16, PADDED), f32),
            pltpu.VMEM((2, 16, PADDED), f32),
            pltpu.VMEM((2, 16, PADDED), f32),
            pltpu.VMEM((2, 16, PADDED), f32),
            pltpu.VMEM((96, 128), f32),
            dma((4,)),
            dma((4,)),
            dma((4,)),
            dma((4,)),
            dma((5,)),
            dma((8,)),
            dma((8,)),
            dma((7,)),
            dma((7,)),
            dma((1,)),
            dma((2,)),
            dma((2,)),
            dma((2,)),
        ],
        compiler_params=pltpu.CompilerParams(
            vmem_limit_bytes=48 * 1024 * 1024, collective_id=0, has_side_effects=True
        ),
    )(spectra, tilt_ranges, table, x_tables)


def solution(mesh):
    cols = mesh.shape["col"]
    inner = functools.partial(body, jnp.asarray(x_table(cols)), jnp.asarray(y_table()))
    return jax.shard_map(
        inner,
        mesh=mesh,
        in_specs=(P("row", None, None, "col"), P("row", None)),
        out_specs=P("row", "col", None),
        check_vma=False,
    )
```

time: 512 us -> 82 us (0.16)
  the two profiles are of different devices: /device:TPU:24 before, /device:TPU:26 now
where the time goes in v1:
time: 82 us; the launch traced here: 81.8 us
  Pallas kernels  76.3 us (93%)
  local copies, waits for them, and re-layouts  5.43 us (7%)
    pallas_call x1, Pallas kernels, body(): pl.pallas_call(fused_kernel, out_shape=jax.ShapeDtypeStruct((4, 8, WINDOW...  76.3 us
    unnamed x7, local copies, waits for them, and re-layouts  5.43 us

profile of v1, /device:TPU:26, one launch (start us, length us, event | category | flops | bytes accessed | tf_op | source)
XLA Modules:
  0.0 81.8 jit_solution(4273603195092587212)
XLA Ops:
  0.0 0.8 copy.6.tilts_any
  0.8 0.9 %copy.5.spectra_any = bf16[4,2,33,256]{3,2,1,0:T(8,128)(2,1)S(1)} copy(bf16[4,2,33,256]{3,1,2,0:T(2,128)(2,1)} %param.4) | data formatting | bytes 270336 | tf_op args[0]
  1.7 0.0 copy-start
  1.7 2.3 %copy-done = bf16[16,576,256]{2,1,0:T(8,128)(2,1)S(1)} copy-done((bf16[16,576,256]{2,1,0:T(8,128)(2,1)S(1)}, bf16[16,576,256]{2,1,0:T(8,128)(2,1)}, u32[]{:S(2)}) %copy-start) | copy-done | bytes 4718616
  4.0 0.0 copy-start.1
  4.0 0.8 copy-done.1
  4.8 76.3 %shard_map.46 = f32[4,8,729]{2,1,0:T(8,128)S(1)} custom-call(bf16[4,2,33,256]{3,2,1,0:T(8,128)(2,1)S(1)} %copy.5.spectra_any, s32[4,2]{1,0:T(4,128)S(1)} %copy.6.tilts_any, f32[9,8,128]{2,1,0:T(8,128)S(1)} %copy-done.1, bf16[16,576,256]{2,1,0:T(8,128)(2,1)S(1)} %copy-done), custom_call_target="tpu_custom_call" | custom-call | tf_op jit(solution)/shard_map/pallas_call | solution.py:512
  81.1 0.6 copy.8
Async XLA Ops:
  1.7 2.3 %copy-start = (bf16[16,576,256]{2,1,0:T(8,128)(2,1)S(1)}, bf16[16,576,256]{2,1,0:T(8,128)(2,1)}, u32[]{:S(2)}) copy-start(bf16[16,576,256]{2,1,0:T(8,128)(2,1)} %constant.5.clone.tables_any) | copy-start | bytes 14155780
  4.0 0.8 copy-start.1

commit v2 on v1

--- a/solution.py
+++ b/solution.py
@@ -18,6 +18,7 @@
 PADDED = 768
 TILES = HALF + 2
 PIECE = 40
+ROWS = 24
 NT = (((1,), (1,)), ((), ()))
 
 
@@ -42,18 +43,18 @@
 
 
 def x_table(cols):
-    out = np.zeros((cols, LAGS, 32, 2, 8, 4, 4), np.float64)
+    out = np.zeros((cols, LAGS, ROWS, 2, 8, 4, 4), np.float64)
     for col in range(cols):
         for k in range(4):
             for lx in range(-REACH, REACH + 1):
                 angle = 2 * np.pi * ((col * 4 + k) * lx % EDGE) / EDGE
-                for r in range(8):
+                for r in range(ROWS // 4):
                     for s in range(4):
                         out[col, lx + REACH, r * 4 + s, 0, r, k, s] = math.cos(angle)
                         out[col, lx + REACH, r * 4 + s, 1, r, k, s] = -math.sin(angle)
-    out = out.reshape(cols, LAGS * 32, 256)
-    high, low = split_np(out)
-    return np.concatenate([high, low], 1)
+    out = out.reshape(cols, LAGS * ROWS, 256)
+    out = np.pad(out, ((0, 0), (0, 224 - LAGS * ROWS), (0, 0)))
+    return np.stack(split_np(out), 1)
 
 
 def z_coefs():
@@ -118,22 +119,26 @@
     def one(z, carry):
         base = block[z].astype(jnp.float32)
         turned = pltpu.roll(base, EDGE, 1)
-        highs, lows = [], []
-        for k in range(4):
-            both = jnp.concatenate([base[4 * k : 4 * k + 4], turned[4 * k : 4 * k + 4]], axis=0)
-            for i in range(LAGS):
-                value = both * table[i]
-                high = value.astype(jnp.bfloat16)
-                highs.append(high)
-                lows.append((value - high.astype(jnp.float32)).astype(jnp.bfloat16))
-        mod[z, :, :128] = jnp.concatenate(highs, axis=0)
-        mod[z, :, 128:] = jnp.concatenate(lows, axis=0)
+        values = []
+        for k in range(0, 4, 2):
+            a, b = base[4 * k : 4 * k + 8], turned[4 * k : 4 * k + 8]
+            for both in (
+                jnp.where(first, a, pltpu.roll(b, 4, 0)),
+                jnp.where(first, pltpu.roll(a, 4, 0), b),
+            ):
+                values += [both * table[i] for i in range(LAGS)]
+        value = jnp.concatenate(values, axis=0)
+        high = value.astype(jnp.bfloat16)
+        mod[z, :, :128] = high
+        mod[z, :, 128:] = (value - high.astype(jnp.float32)).astype(jnp.bfloat16)
         return carry
 
-    lax.fori_loop(0, HALF, one, 0, unroll=3)
-
-
-def window_tile(own, mod, blocks, depth, quads):
+    first = lax.broadcasted_iota(jnp.int32, (8, 128), 0) < 4
+
+    lax.fori_loop(0, HALF, one, 0, unroll=11)
+
+
+def window_tile(own, mod, blocks, depth, quads, middle):
     lane_k = (lax.broadcasted_iota(jnp.int32, (8, 128), 1) // 4) % 4
 
     def diagonal(values):
@@ -153,6 +158,7 @@
 
     lax.fori_loop(0, HALF, one, 0, unroll=11)
 
+    middle()
     energies = []
     for own_tile, other in ((HALF, HALF + 1), (HALF + 1, HALF)):
         product = lax.dot_general(own[own_tile], blocks(other), NT, preferred_element_type=jnp.float32)
@@ -228,13 +234,31 @@
     value = jnp.concatenate([real, imag], axis=1)
     high = value.astype(jnp.bfloat16)
     low = (value - high.astype(jnp.float32)).astype(jnp.bfloat16)
-    x_high, x_low = xt[:288], xt[288:]
+    x_high, x_low = xt[0], xt[1]
     dot = functools.partial(lax.dot_general, dimension_numbers=NT, preferred_element_type=jnp.float32)
     out = dot(x_high, high) + (dot(x_low, high) + dot(x_high, low))
-    pieces = [out[32 * i : 32 * i + 32, :81] for i in range(LAGS)]
-    energy = out[32 * REACH : 32 * REACH + 32, 81:83]
-    fill = jnp.zeros((32, PADDED - WINDOW - 2), jnp.float32)
+    pieces = [out[ROWS * i : ROWS * i + ROWS, :81] for i in range(LAGS)]
+    energy = out[ROWS * REACH : ROWS * REACH + ROWS, 81:83]
+    fill = jnp.zeros((ROWS, PADDED - WINDOW - 2), jnp.float32)
     return jnp.concatenate(pieces + [energy, fill], axis=1)
+
+
+def write_part(x, xx, yy, order, xt, part):
+    first = lax.broadcasted_iota(jnp.int32, (8, PADDED), 0) < 4
+    for pair in range(2):
+        a, b = window_out(order, xt, 2 * pair), window_out(order, xt, 2 * pair + 1)
+        blocks = []
+        for i in range(0, ROWS, 8):
+            upper, lower = a[i : i + 8], b[i : i + 8]
+            blocks.append(jnp.where(first, upper, pltpu.roll(lower, 4, 0)))
+            blocks.append(jnp.where(first, pltpu.roll(upper, 4, 0), lower))
+        for y in range(4):
+            swap = (yy == y) & (x < xx)
+            part[x * 4 + y, 8 * pair : 8 * pair + 8, :] = jnp.where(swap, blocks[4], blocks[y])
+
+        @pl.when(x == xx)
+        def _():
+            part[16, 8 * pair : 8 * pair + 8, :] = blocks[4]
 
 
 def flip_rows(rows):
@@ -255,7 +279,7 @@
 def fused_kernel(
     spectra_any, tilts_any, table_any, tables_any, out,
     spectra, tilts, table, xt, power, pieces, own, mods, lanes, mod, depth, quads, order,
-    part, extra, from_left, from_right, extra_in, sent, final, turned,
+    part, from_left, from_right, extra_in, sent, final, turned,
     local_sem, x_send, x_recv, y_send, y_recv, right_send, right_recv, left_send, left_recv,
     extra_send, extra_recv, final_send, final_recv,
 ):
@@ -313,14 +337,13 @@
         )
 
     gathers = []
-    for i in range(1, 4):
+    for i in (1, 3, 2):
         y = lax.rem(yy + i, 4)
         there = jnp.where(y < yy, core, 1 - core)
         gathers.append(remote(own, lanes.at[yy], y_send.at[i], y_recv.at[yy], at(xx, y, there, z)))
-    gathers.append(remote(own, lanes.at[4], y_send.at[0], y_recv.at[4], at(xx, yy, 1 - core, z)))
-    for i in range(1, 4):
         x = lax.rem(xx + i, 4)
         gathers.append(remote(own, mods.at[xx], x_send.at[i], x_recv.at[xx], at(x, yy, core, z)))
+    gathers.append(remote(own, lanes.at[4], y_send.at[0], y_recv.at[4], at(xx, yy, 1 - core, z)))
     for copy in gathers:
         copy.start()
 
@@ -348,10 +371,10 @@
 
         @pl.when(chunk == chip)
         def _():
-            copy = remote(extra, extra_in.at[0], extra_send.at[0], extra_recv.at[0], at(xx, yy, core, right))
+            copy = remote(part.at[16], extra_in.at[0], extra_send.at[0], extra_recv.at[0], at(xx, yy, core, right))
             if step > 1:
                 copy.wait_recv()
-                extra[...] = extra[...] + extra_in[0]
+                part[16] = part[16] + extra_in[0]
             copy.start()
 
     def move_left(step):
@@ -364,10 +387,10 @@
 
         @pl.when(chunk == chip)
         def _():
-            copy = remote(extra, extra_in.at[1], extra_send.at[0], extra_recv.at[1], at(xx, yy, core, left))
+            copy = remote(part.at[16], extra_in.at[1], extra_send.at[0], extra_recv.at[1], at(xx, yy, core, left))
             if step > 1:
                 copy.wait_recv()
-                extra[...] = extra[...] + extra_in[1]
+                part[16] = part[16] + extra_in[1]
             copy.start()
 
     second = jnp.where(zy < 2, 1, 3)
@@ -381,21 +404,19 @@
             remote(own, mods.at[x], x_send.at[0], x_recv.at[x], at(xx, yy, 1 - core, z)).wait_recv()
             modulate(mods.at[x], table, mod.at[1])
 
+        def middle():
+            for at_q, step in ((2, 3), (3, 5)):
+                @pl.when(q == at_q)
+                def _():
+                    move_right(step)
+                    move_left(step - 1)
+
         def blocks(k):
             return lanes[:, k].reshape(128, 128)
 
-        rows = window_tile(mods.at[x], mod.at[jnp.where(x == xx, 0, 1)], blocks, depth, quads)
+        rows = window_tile(mods.at[x], mod.at[jnp.where(x == xx, 0, 1)], blocks, depth, quads, middle)
         order[...] = jnp.concatenate(rows, axis=0)
-        for s in range(4):
-            value = window_out(order, xt, s)
-            other = value[16:20]
-            for y in range(4):
-                swap = (yy == y) & (x < xx)
-                part[x * 4 + y, 4 * s : 4 * s + 4, :] = jnp.where(swap, other, value[4 * y : 4 * y + 4])
-
-            @pl.when(x == xx)
-            def _():
-                extra[4 * s : 4 * s + 4, :] = other
+        write_part(x, xx, yy, order, xt, part)
 
         @pl.when(q == 0)
         def _():
@@ -403,15 +424,13 @@
 
         @pl.when(q == 1)
         def _():
-            for step in (2, 3):
-                move_right(step)
-                move_left(step - 1)
+            move_right(2)
+            move_left(1)
 
         @pl.when(q == 2)
         def _():
-            for step in (4, 5):
-                move_right(step)
-                move_left(step - 1)
+            move_right(4)
+            move_left(3)
 
         return carry
 
@@ -463,8 +482,8 @@
     @pl.when(home)
     def _():
         for i, send in ((0, right), (1, left)):
-            remote(extra, extra_in.at[i], extra_send.at[0], extra_recv.at[i], at(xx, yy, core, send)).wait_recv()
-        final[1] = scaled(extra[...] + extra_in[0] + extra_in[1])
+            remote(part.at[16], extra_in.at[i], extra_send.at[0], extra_recv.at[i], at(xx, yy, core, send)).wait_recv()
+        final[1] = scaled(part[16] + extra_in[0] + extra_in[1])
 
     @pl.when(jnp.logical_not(same_x))
     def _():
@@ -502,7 +521,7 @@
 
     @pl.when(jnp.logical_not(home))
     def _():
-        remote(extra, extra_in.at[0], extra_send.at[0], extra_recv.at[0], at(xx, yy, core, right)).wait_send()
+        remote(part.at[16], extra_in.at[0], extra_send.at[0], extra_recv.at[0], at(xx, yy, core, right)).wait_send()
 
 
 def body(x_tables, table, spectra, tilt_ranges):
@@ -518,7 +537,7 @@
             pltpu.VMEM((4, 2, HALF, 256), bf16),
             pltpu.SMEM((4, 2), jnp.int32),
             pltpu.VMEM((LAGS, 8, 128), f32),
-            pltpu.VMEM((576, 256), bf16),
+            pltpu.VMEM((2, 224, 256), bf16),
             pltpu.VMEM((128, 256), f32),
             pltpu.VMEM((HALF, 16, 128), f32),
             pltpu.VMEM((TILES, 16, 128), bf16),
@@ -528,8 +547,7 @@
             pltpu.VMEM((HALF, LAGS, 8, 128), f32),
             pltpu.VMEM((LAGS, LAGS, 8, 128), f32),
             pltpu.VMEM((88 * 8, 128), f32),
-            pltpu.VMEM((16, 16, PADDED), f32),
-            pltpu.VMEM((16, PADDED), f32),
+            pltpu.VMEM((17, 16, PADDED), f32),
             pltpu.VMEM((8, 16, PADDED), f32),
             pltpu.VMEM((7, 16, PADDED), f32),
             pltpu.VMEM((2, 16, PADDED), f32),
@@ -551,7 +569,7 @@
             dma((2,)),
         ],
         compiler_params=pltpu.CompilerParams(
-            vmem_limit_bytes=48 * 1024 * 1024, collective_id=0, has_side_effects=True
+            vmem_limit_bytes=60 * 1024 * 1024, collective_id=0, has_side_effects=True
         ),
     )(spectra, tilt_ranges, table, x_tables)
 

time: 82 us -> 71 us (0.87)
  the two profiles are of different devices: /device:TPU:26 before, /device:TPU:36 now
where the time goes in v2:
time: 71 us; the launch traced here: 70.8 us
  Pallas kernels  66.3 us (93%)
  local copies, waits for them, and re-layouts  4.45 us (6%)
    pallas_call x1, Pallas kernels, body(): pl.pallas_call(fused_kernel, out_shape=jax.ShapeDtypeStruct((4, 8, WINDOW...  66.3 us
    unnamed x3, local copies, waits for them, and re-layouts  4.45 us

profile of v2, /device:TPU:36, one launch (start us, length us, event | category | flops | bytes accessed | tf_op | source)
XLA Modules:
  0.0 70.8 jit_solution(1770219464118747595)
XLA Ops:
  0.0 1.3 %copy.6.tilts_any = s32[4,2]{1,0:T(4,128)} copy(s32[4,2]{0,1:T(2,128)} %param.5) | data formatting | bytes 64 | tf_op args[1]
  1.3 1.6 %copy.5.spectra_any = bf16[4,2,33,256]{3,2,1,0:T(8,128)(2,1)} copy(bf16[4,2,33,256]{3,1,2,0:T(2,128)(2,1)} %param.4) | data formatting | bytes 270336 | tf_op args[0]
  2.9 66.3 %shard_map.46 = f32[4,8,729]{2,1,0:T(8,128)} custom-call(bf16[4,2,33,256]{3,2,1,0:T(8,128)(2,1)} %copy.5.spectra_any, s32[4,2]{1,0:T(4,128)} %copy.6.tilts_any, f32[9,8,128]{2,1,0:T(8,128)} %constant.4.clone.table_any, bf16[16,2,224,256]{3,2,1,0:T(8,128)(2,1)} %constant.5.clone.tables_any), custom_call_target="tpu_custom_call" | custom-call | tf_op jit(solution)/shard_map/pallas_call | solution.py:531
  69.3 1.5 %copy.8 = f32[4,8,729]{2,1,0:T(8,128)} copy(f32[4,8,729]{2,1,0:T(8,128)} %shard_map.46) | data formatting | bytes 186624

commit v3 on v2

--- a/solution.py
+++ b/solution.py
@@ -83,7 +83,7 @@
     lane = lax.broadcasted_iota(jnp.int32, (16, 256), 1)
     total = jnp.zeros((16, 128), jnp.float32)
     for s in range(4):
-        mask = observed(freq_z, freq_x, tilts[s, 0], tilts[s, 1])
+        mask = observed(freq_z, freq_x, tilts[0, s], tilts[1, s])
         real = jnp.where(mask, spectra[s, 0].astype(jnp.float32), 0.0)
         imag = jnp.where(mask, spectra[s, 1].astype(jnp.float32), 0.0)
         square = (real * real + imag * imag) * weight
@@ -107,7 +107,7 @@
     message[HALF] = jnp.where(third == 0, high, jnp.where(third == 1, mid, low)).astype(jnp.bfloat16)
     s = row % 4
     up, down = (
-        jnp.where(s == 0, tilts[0, i], jnp.where(s == 1, tilts[1, i], jnp.where(s == 2, tilts[2, i], tilts[3, i])))
+        jnp.where(s == 0, tilts[i, 0], jnp.where(s == 1, tilts[i, 1], jnp.where(s == 2, tilts[i, 2], tilts[i, 3])))
         for i in range(2)
     )
     at = lane - third * PIECE
@@ -279,9 +279,9 @@
 def fused_kernel(
     spectra_any, tilts_any, table_any, tables_any, out,
     spectra, tilts, table, xt, power, pieces, own, mods, lanes, mod, depth, quads, order,
-    part, from_left, from_right, extra_in, sent, final, turned,
-    local_sem, x_send, x_recv, y_send, y_recv, right_send, right_recv, left_send, left_recv,
-    extra_send, extra_recv, final_send, final_recv,
+    part, merge, chain, extra_merge, extra_chain, sent, final, turned,
+    local_sem, x_send, x_recv, y_send, y_recv, merge_send, merge_recv, chain_send, chain_recv,
+    extra_send, extra_merge_recv, extra_chain_recv, final_send, final_recv,
 ):
     row = lax.axis_index("row")
     z = lax.axis_index("col")
@@ -291,6 +291,9 @@
 
     def at(x, y, c, depth_z):
         return {"row": (x * 4 + y) * 2 + c, "col": depth_z}
+
+    def along(offset):
+        return at(xx, yy, core, lax.rem(z + offset, 16))
 
     locals_ = [
         pltpu.make_async_copy(spectra_any, spectra, local_sem.at[0]),
@@ -311,9 +314,8 @@
         greet(at(xx, lax.rem(yy + i, 4), 0, z))
         greet(at(xx, lax.rem(yy + i, 4), 1, z))
     greet(at(xx, yy, 1 - core, z))
-    right, left = lax.rem(z + 1, 16), lax.rem(z + 15, 16)
-    greet(at(xx, yy, core, right))
-    greet(at(xx, yy, core, left))
+    for offset in (1, 15, 2, 14):
+        greet(along(offset))
 
     @pl.when(zx != xx)
     def _():
@@ -327,7 +329,7 @@
     locals_[0].wait()
     locals_[1].wait()
     prepare(z, spectra, tilts, own, power, pieces)
-    count = 12 + jnp.where(zx != xx, 1, 0) + jnp.where(zy != yy, 2, 0)
+    count = 14 + jnp.where(zx != xx, 1, 0) + jnp.where(zy != yy, 2, 0)
     pl.semaphore_wait(barrier, count)
 
     def remote(src, dst, send, recv, target):
@@ -337,13 +339,14 @@
         )
 
     gathers = []
-    for i in (1, 3, 2):
+    for i in (2, 1, 3):
         y = lax.rem(yy + i, 4)
         there = jnp.where(y < yy, core, 1 - core)
         gathers.append(remote(own, lanes.at[yy], y_send.at[i], y_recv.at[yy], at(xx, y, there, z)))
+    gathers.append(remote(own, lanes.at[4], y_send.at[0], y_recv.at[4], at(xx, yy, 1 - core, z)))
+    for i in (1, 3, 2):
         x = lax.rem(xx + i, 4)
         gathers.append(remote(own, mods.at[xx], x_send.at[i], x_recv.at[xx], at(x, yy, core, z)))
-    gathers.append(remote(own, lanes.at[4], y_send.at[0], y_recv.at[4], at(xx, yy, 1 - core, z)))
     for copy in gathers:
         copy.start()
 
@@ -361,37 +364,64 @@
         wait_lane(lax.rem(yy + i, 4))
     wait_lane(4)
 
-    def move_right(step):
-        chunk = lax.rem(z + 9 - step, 16)
-        if step > 1:
-            before = remote(part.at[chunk], from_left.at[step - 2], right_send.at[step - 2], right_recv.at[step - 2], at(xx, yy, core, right))
-            before.wait_recv()
-            part[chunk] = part[chunk] + from_left[step - 2]
-        remote(part.at[chunk], from_left.at[step - 1], right_send.at[step - 1], right_recv.at[step - 1], at(xx, yy, core, right)).start()
+    near_hop, far_hop = (1, 15), (2, 14)
+
+    def merging(side, i, chunk):
+        return remote(
+            part.at[chunk], merge.at[side, i], merge_send.at[side, i], merge_recv.at[side, i], along(near_hop[side])
+        )
+
+    def chaining(side, i, chunk):
+        return remote(
+            part.at[chunk], chain.at[side, i], chain_send.at[side, i], chain_recv.at[side, i], along(far_hop[side])
+        )
+
+    def extra_merging(side):
+        return remote(
+            part.at[16], extra_merge.at[side], extra_send.at[0], extra_merge_recv.at[side], along(near_hop[side])
+        )
+
+    def extra_chaining(side):
+        return remote(
+            part.at[16], extra_chain.at[side], extra_send.at[0], extra_chain_recv.at[side], along(far_hop[side])
+        )
+
+    def spread(x):
+        for k in range(4):
+            chunk = x * 4 + k
+            ahead = lax.rem(chunk + 16 - z, 16)
+            odd = lax.rem(ahead, 2) == 1
+            for side, here, gap in ((0, odd & (ahead < 8), ahead), (1, odd & (ahead > 8), 16 - ahead)):
+                @pl.when(here)
+                def _():
+                    merging(side, gap // 2, chunk).start()
+
+                    @pl.when(chunk == chip)
+                    def _():
+                        extra_merging(side).start()
+
+    def step(side, gap):
+        longest = 8 - 2 * side
+        chunk = lax.rem(z + (gap, 16 - gap)[side], 16)
+        order_at = (longest - gap) // 2
+        merged, chained = gap < 8, gap < longest
+        if merged:
+            merging(side, gap // 2, chunk).wait_recv()
+            part[chunk] = part[chunk] + merge[side, gap // 2]
+        if chained:
+            chaining(side, order_at - 1, chunk).wait_recv()
+            part[chunk] = part[chunk] + chain[side, order_at - 1]
+        chaining(side, order_at, chunk).start()
 
         @pl.when(chunk == chip)
         def _():
-            copy = remote(part.at[16], extra_in.at[0], extra_send.at[0], extra_recv.at[0], at(xx, yy, core, right))
-            if step > 1:
-                copy.wait_recv()
-                part[16] = part[16] + extra_in[0]
-            copy.start()
-
-    def move_left(step):
-        chunk = lax.rem(z + 8 + step, 16)
-        if step > 1:
-            before = remote(part.at[chunk], from_right.at[step - 2], left_send.at[step - 2], left_recv.at[step - 2], at(xx, yy, core, left))
-            before.wait_recv()
-            part[chunk] = part[chunk] + from_right[step - 2]
-        remote(part.at[chunk], from_right.at[step - 1], left_send.at[step - 1], left_recv.at[step - 1], at(xx, yy, core, left)).start()
-
-        @pl.when(chunk == chip)
-        def _():
-            copy = remote(part.at[16], extra_in.at[1], extra_send.at[0], extra_recv.at[1], at(xx, yy, core, left))
-            if step > 1:
-                copy.wait_recv()
-                part[16] = part[16] + extra_in[1]
-            copy.start()
+            if merged:
+                extra_merging(side).wait_recv()
+                part[16] = part[16] + extra_merge[side]
+            if chained:
+                extra_chaining(side).wait_recv()
+                part[16] = part[16] + extra_chain[side]
+            extra_chaining(side).start()
 
     second = jnp.where(zy < 2, 1, 3)
 
@@ -405,11 +435,11 @@
             modulate(mods.at[x], table, mod.at[1])
 
         def middle():
-            for at_q, step in ((2, 3), (3, 5)):
+            for at_q, gap in ((2, 6), (3, 4)):
                 @pl.when(q == at_q)
                 def _():
-                    move_right(step)
-                    move_left(step - 1)
+                    step(0, gap)
+                    step(1, gap)
 
         def blocks(k):
             return lanes[:, k].reshape(128, 128)
@@ -418,33 +448,25 @@
         order[...] = jnp.concatenate(rows, axis=0)
         write_part(x, xx, yy, order, xt, part)
 
+        spread(x)
+
         @pl.when(q == 0)
         def _():
-            move_right(1)
-
-        @pl.when(q == 1)
-        def _():
-            move_right(2)
-            move_left(1)
-
-        @pl.when(q == 2)
-        def _():
-            move_right(4)
-            move_left(3)
+            step(0, 8)
 
         return carry
 
     lax.fori_loop(0, 4, task, 0)
-    for step in (6, 7, 8):
-        move_right(step)
-        move_left(step - 1)
-    remote(part.at[z], from_left.at[7], right_send.at[7], right_recv.at[7], at(xx, yy, core, right)).wait_recv()
-    remote(part.at[z], from_right.at[6], left_send.at[6], left_recv.at[6], at(xx, yy, core, left)).wait_recv()
+    step(0, 2)
+    step(1, 2)
+    for side in range(2):
+        merging(side, 0, z).wait_recv()
+        chaining(side, 3 - side, z).wait_recv()
 
     def scaled(total):
         return total / jnp.sqrt(total[:, WINDOW : WINDOW + 1] * total[:, WINDOW + 1 : WINDOW + 2])
 
-    value = scaled(part[z] + from_left[7] + from_right[6])
+    value = scaled(part[z] + (merge[0, 0] + merge[1, 0]) + (chain[0, 3] + chain[1, 2]))
     same_x = zx == xx
     home = z == chip
     keep = (zy == yy) & (zx >= xx)
@@ -481,9 +503,10 @@
 
     @pl.when(home)
     def _():
-        for i, send in ((0, right), (1, left)):
-            remote(part.at[16], extra_in.at[i], extra_send.at[0], extra_recv.at[i], at(xx, yy, core, send)).wait_recv()
-        final[1] = scaled(part[16] + extra_in[0] + extra_in[1])
+        for side in range(2):
+            extra_merging(side).wait_recv()
+            extra_chaining(side).wait_recv()
+        final[1] = scaled(part[16] + (extra_merge[0] + extra_merge[1]) + (extra_chain[0] + extra_chain[1]))
 
     @pl.when(jnp.logical_not(same_x))
     def _():
@@ -514,14 +537,15 @@
 
     for copy in gathers:
         copy.wait_send()
-    for i in range(8):
-        remote(part.at[i], from_left.at[i], right_send.at[i], right_recv.at[i], at(xx, yy, core, right)).wait_send()
-    for i in range(7):
-        remote(part.at[i], from_right.at[i], left_send.at[i], left_recv.at[i], at(xx, yy, core, left)).wait_send()
+    for side in range(2):
+        for i in range(4):
+            merging(side, i, z).wait_send()
+        for i in range(4 - side):
+            chaining(side, i, z).wait_send()
 
     @pl.when(jnp.logical_not(home))
     def _():
-        remote(part.at[16], extra_in.at[0], extra_send.at[0], extra_recv.at[0], at(xx, yy, core, right)).wait_send()
+        extra_merging(0).wait_send()
 
 
 def body(x_tables, table, spectra, tilt_ranges):
@@ -535,7 +559,7 @@
         out_specs=pl.BlockSpec(memory_space=pltpu.VMEM),
         scratch_shapes=[
             pltpu.VMEM((4, 2, HALF, 256), bf16),
-            pltpu.SMEM((4, 2), jnp.int32),
+            pltpu.SMEM((2, 4), jnp.int32),
             pltpu.VMEM((LAGS, 8, 128), f32),
             pltpu.VMEM((2, 224, 256), bf16),
             pltpu.VMEM((128, 256), f32),
@@ -548,8 +572,9 @@
             pltpu.VMEM((LAGS, LAGS, 8, 128), f32),
             pltpu.VMEM((88 * 8, 128), f32),
             pltpu.VMEM((17, 16, PADDED), f32),
-            pltpu.VMEM((8, 16, PADDED), f32),
-            pltpu.VMEM((7, 16, PADDED), f32),
+            pltpu.VMEM((2, 4, 16, PADDED), f32),
+            pltpu.VMEM((2, 4, 16, PADDED), f32),
+            pltpu.VMEM((2, 16, PADDED), f32),
             pltpu.VMEM((2, 16, PADDED), f32),
             pltpu.VMEM((2, 16, PADDED), f32),
             pltpu.VMEM((2, 16, PADDED), f32),
@@ -559,11 +584,12 @@
             dma((4,)),
             dma((4,)),
             dma((5,)),
-            dma((8,)),
-            dma((8,)),
-            dma((7,)),
-            dma((7,)),
+            dma((2, 4)),
+            dma((2, 4)),
+            dma((2, 4)),
+            dma((2, 4)),
             dma((1,)),
+            dma((2,)),
             dma((2,)),
             dma((2,)),
             dma((2,)),
@@ -571,7 +597,7 @@
         compiler_params=pltpu.CompilerParams(
             vmem_limit_bytes=60 * 1024 * 1024, collective_id=0, has_side_effects=True
         ),
-    )(spectra, tilt_ranges, table, x_tables)
+    )(spectra, tilt_ranges.T, table, x_tables)
 
 
 def solution(mesh):

time: 71 us -> 66.2 us (0.932)
  the two profiles are of different devices: /device:TPU:36 before, /device:TPU:24 now
where the time goes in v3:
time: 66.2 us; the launch traced here: 66.1 us
  Pallas kernels  62.9 us (95%)
  local copies, waits for them, and re-layouts  3.11 us (5%)
    pallas_call x1, Pallas kernels, body(): pl.pallas_call(fused_kernel, out_shape=jax.ShapeDtypeStruct((4, 8, WINDOW...  62.9 us
    unnamed x2, local copies, waits for them, and re-layouts  3.11 us

profile of v3, /device:TPU:24, one launch (start us, length us, event | category | flops | bytes accessed | tf_op | source)
XLA Modules:
  0.0 66.1 jit_solution(13800648188696457440)
XLA Ops:
  0.0 1.6 %copy.5.spectra_any = bf16[4,2,33,256]{3,2,1,0:T(8,128)(2,1)} copy(bf16[4,2,33,256]{3,1,2,0:T(2,128)(2,1)} %param.4) | data formatting | bytes 270336 | tf_op args[0]
  1.6 62.9 %shard_map.46 = f32[4,8,729]{2,1,0:T(8,128)} custom-call(bf16[4,2,33,256]{3,2,1,0:T(8,128)(2,1)} %copy.5.spectra_any, s32[2,4]{1,0:T(2,128)} %bitcast.1, f32[9,8,128]{2,1,0:T(8,128)} %constant.4.clone.table_any, bf16[16,2,224,256]{3,2,1,0:T(8,128)(2,1)} %constant.5.clone.tables_any), custom_call_target="tpu_custom_call" | custom-call | tf_op jit(solution)/shard_map/pallas_call | solution.py:555
  64.5 1.5 %copy.7 = f32[4,8,729]{2,1,0:T(8,128)} copy(f32[4,8,729]{2,1,0:T(8,128)} %shard_map.46) | data formatting | bytes 186624

commit v4 on v3

--- a/solution.py
+++ b/solution.py
@@ -18,6 +18,8 @@
 PADDED = 768
 TILES = HALF + 2
 PIECE = 40
+PARTS = ((0, 22), (22, HALF))
+SPANS = ((0, 22), (22, TILES))
 ROWS = 24
 NT = (((1,), (1,)), ((), ()))
 
@@ -73,30 +75,37 @@
     return 16 * freq_z <= jnp.where(q > 0, up, down) * jnp.abs(q)
 
 
-def prepare(col, spectra, tilts, message, power, pieces):
+def prepare_first(col, spectra, tilts, message, squares, pieces):
     lanes = lax.broadcasted_iota(jnp.int32, (HALF, 256), 1)
     freq_z = lax.broadcasted_iota(jnp.int32, (HALF, 256), 0)
     freq_x = col * 4 + lanes // EDGE
     weight = jnp.where((freq_z == 0) | (freq_z == EDGE // 2), 1.0, 2.0).astype(jnp.float32)
+    for s in range(4):
+        mask = observed(freq_z, freq_x, tilts[0, s], tilts[1, s])
+        real = jnp.where(mask, spectra[s, 0].astype(jnp.float32), 0.0)
+        imag = jnp.where(mask, spectra[s, 1].astype(jnp.float32), 0.0)
+        squares[s] = (real * real + imag * imag) * weight
+        for k in range(4):
+            part = slice(k * EDGE, (k + 1) * EDGE)
+            pieces[:, k * 4 + s, :] = jnp.concatenate([real[:, part], imag[:, part]], axis=1)
+    first, last = PARTS[0]
+    message[first:last] = pieces[first:last].astype(jnp.bfloat16)
+
+
+def prepare_second(col, tilts, message, squares, power, pieces):
+    first, last = PARTS[1]
+    message[first:last] = pieces[first:last].astype(jnp.bfloat16)
     power[...] = jnp.zeros_like(power)
     row = lax.broadcasted_iota(jnp.int32, (16, 256), 0)
     lane = lax.broadcasted_iota(jnp.int32, (16, 256), 1)
     total = jnp.zeros((16, 128), jnp.float32)
     for s in range(4):
-        mask = observed(freq_z, freq_x, tilts[0, s], tilts[1, s])
-        real = jnp.where(mask, spectra[s, 0].astype(jnp.float32), 0.0)
-        imag = jnp.where(mask, spectra[s, 1].astype(jnp.float32), 0.0)
-        square = (real * real + imag * imag) * weight
         for p in range(3):
-            power[PIECE * p : PIECE * p + HALF, :] = square
+            power[PIECE * p : PIECE * p + HALF, :] = squares[s]
         chosen = jnp.where((row // 4 == lane // EDGE) & (row % 4 == s), 1.0, 0.0)
         total = total + lax.dot_general(
             chosen, power[...], NT, precision=lax.Precision.HIGHEST, preferred_element_type=jnp.float32
         )
-        for k in range(4):
-            part = slice(k * EDGE, (k + 1) * EDGE)
-            pieces[:, k * 4 + s, :] = jnp.concatenate([real[:, part], imag[:, part]], axis=1)
-    message[:HALF] = pieces[...].astype(jnp.bfloat16)
     lane = lax.broadcasted_iota(jnp.int32, (16, 128), 1)
     row = lax.broadcasted_iota(jnp.int32, (16, 128), 0)
     high = total.astype(jnp.bfloat16).astype(jnp.float32)
@@ -115,7 +124,7 @@
     message[HALF + 1] = jnp.where(mask, 1.0, 0.0).astype(jnp.bfloat16)
 
 
-def modulate(block, table, mod):
+def modulate(block, table, mod, part):
     def one(z, carry):
         base = block[z].astype(jnp.float32)
         turned = pltpu.roll(base, EDGE, 1)
@@ -135,10 +144,10 @@
 
     first = lax.broadcasted_iota(jnp.int32, (8, 128), 0) < 4
 
-    lax.fori_loop(0, HALF, one, 0, unroll=11)
-
-
-def window_tile(own, mod, blocks, depth, quads, middle):
+    lax.fori_loop(*part, one, 0, unroll=11)
+
+
+def window_tile(own, mod, blocks, depth, quads, middle, ready):
     lane_k = (lax.broadcasted_iota(jnp.int32, (8, 128), 1) // 4) % 4
 
     def diagonal(values):
@@ -156,7 +165,9 @@
         depth[z] = diagonal([product[72 * k : 72 * k + 72] for k in range(4)]).reshape(LAGS, 8, 128)
         return carry
 
-    lax.fori_loop(0, HALF, one, 0, unroll=11)
+    for i, part in enumerate(PARTS):
+        ready(i)
+        lax.fori_loop(*part, one, 0, unroll=11)
 
     middle()
     energies = []
@@ -278,7 +289,7 @@
 
 def fused_kernel(
     spectra_any, tilts_any, table_any, tables_any, out,
-    spectra, tilts, table, xt, power, pieces, own, mods, lanes, mod, depth, quads, order,
+    spectra, tilts, table, xt, squares, power, pieces, own, mods, lanes, mod, depth, quads, order,
     part, merge, chain, extra_merge, extra_chain, sent, final, turned,
     local_sem, x_send, x_recv, y_send, y_recv, merge_send, merge_recv, chain_send, chain_recv,
     extra_send, extra_merge_recv, extra_chain_recv, final_send, final_recv,
@@ -328,7 +339,7 @@
 
     locals_[0].wait()
     locals_[1].wait()
-    prepare(z, spectra, tilts, own, power, pieces)
+    prepare_first(z, spectra, tilts, own, squares, pieces)
     count = 14 + jnp.where(zx != xx, 1, 0) + jnp.where(zy != yy, 2, 0)
     pl.semaphore_wait(barrier, count)
 
@@ -339,30 +350,41 @@
         )
 
     gathers = []
-    for i in (2, 1, 3):
-        y = lax.rem(yy + i, 4)
-        there = jnp.where(y < yy, core, 1 - core)
-        gathers.append(remote(own, lanes.at[yy], y_send.at[i], y_recv.at[yy], at(xx, y, there, z)))
-    gathers.append(remote(own, lanes.at[4], y_send.at[0], y_recv.at[4], at(xx, yy, 1 - core, z)))
-    for i in (1, 3, 2):
-        x = lax.rem(xx + i, 4)
-        gathers.append(remote(own, mods.at[xx], x_send.at[i], x_recv.at[xx], at(x, yy, core, z)))
-    for copy in gathers:
-        copy.start()
+    for i, span in enumerate(SPANS):
+        if i == 1:
+            prepare_second(z, tilts, own, squares, power, pieces)
+        span = slice(*span)
+        ready_now = []
+        for n in (2, 1, 3):
+            y = lax.rem(yy + n, 4)
+            there = jnp.where(y < yy, core, 1 - core)
+            ready_now.append(
+                remote(own.at[span], lanes.at[yy, span], y_send.at[i, n], y_recv.at[i, yy], at(xx, y, there, z))
+            )
+        ready_now.append(
+            remote(own.at[span], lanes.at[4, span], y_send.at[i, 0], y_recv.at[i, 4], at(xx, yy, 1 - core, z))
+        )
+        for n in (1, 3, 2):
+            x = lax.rem(xx + n, 4)
+            ready_now.append(
+                remote(own.at[span], mods.at[xx, span], x_send.at[i, n], x_recv.at[i, xx], at(x, yy, core, z))
+            )
+        for copy in ready_now:
+            copy.start()
+        gathers += ready_now
 
     lanes[yy] = own[...]
     mods[xx] = own[...]
     lanes[5:8] = jnp.zeros((3, TILES, 16, 128), jnp.bfloat16)
     locals_[2].wait()
-    modulate(own, table, mod.at[0])
+    modulate(own, table, mod.at[0], (0, HALF))
     locals_[3].wait()
 
-    def wait_lane(slot):
-        remote(own, lanes.at[slot], y_send.at[0], y_recv.at[slot], at(xx, yy, 1 - core, z)).wait_recv()
-
-    for i in range(1, 4):
-        wait_lane(lax.rem(yy + i, 4))
-    wait_lane(4)
+    def wait_lane(i, slot):
+        span = slice(*SPANS[i])
+        remote(
+            own.at[span], lanes.at[slot, span], y_send.at[i, 0], y_recv.at[i, slot], at(xx, yy, 1 - core, z)
+        ).wait_recv()
 
     near_hop, far_hop = (1, 15), (2, 14)
 
@@ -429,10 +451,20 @@
         turn = jnp.where(q == 0, 2, jnp.where(q == 1, second, jnp.where(q == 2, 4 - second, 0)))
         x = lax.rem(zx + turn, 4)
 
-        @pl.when(x != xx)
-        def _():
-            remote(own, mods.at[x], x_send.at[0], x_recv.at[x], at(xx, yy, 1 - core, z)).wait_recv()
-            modulate(mods.at[x], table, mod.at[1])
+        def ready(i):
+            @pl.when(x != xx)
+            def _():
+                span = slice(*SPANS[i])
+                remote(
+                    own.at[span], mods.at[x, span], x_send.at[i, 0], x_recv.at[i, x], at(xx, yy, 1 - core, z)
+                ).wait_recv()
+                modulate(mods.at[x], table, mod.at[1], PARTS[i])
+
+            @pl.when(q == 0)
+            def _():
+                for n in range(1, 4):
+                    wait_lane(i, lax.rem(yy + n, 4))
+                wait_lane(i, 4)
 
         def middle():
             for at_q, gap in ((2, 6), (3, 4)):
@@ -444,7 +476,7 @@
         def blocks(k):
             return lanes[:, k].reshape(128, 128)
 
-        rows = window_tile(mods.at[x], mod.at[jnp.where(x == xx, 0, 1)], blocks, depth, quads, middle)
+        rows = window_tile(mods.at[x], mod.at[jnp.where(x == xx, 0, 1)], blocks, depth, quads, middle, ready)
         order[...] = jnp.concatenate(rows, axis=0)
         write_part(x, xx, yy, order, xt, part)
 
@@ -562,6 +594,7 @@
             pltpu.SMEM((2, 4), jnp.int32),
             pltpu.VMEM((LAGS, 8, 128), f32),
             pltpu.VMEM((2, 224, 256), bf16),
+            pltpu.VMEM((4, HALF, 256), f32),
             pltpu.VMEM((128, 256), f32),
             pltpu.VMEM((HALF, 16, 128), f32),
             pltpu.VMEM((TILES, 16, 128), bf16),
@@ -580,10 +613,10 @@
             pltpu.VMEM((2, 16, PADDED), f32),
             pltpu.VMEM((96, 128), f32),
             dma((4,)),
-            dma((4,)),
-            dma((4,)),
-            dma((4,)),
-            dma((5,)),
+            dma((2, 4)),
+            dma((2, 4)),
+            dma((2, 4)),
+            dma((2, 5)),
             dma((2, 4)),
             dma((2, 4)),
             dma((2, 4)),

time: 66.2 us -> 64 us (0.967)
  Pallas kernels: 62.9 us -> 60.7 us
    pallas_call x1, Pallas kernels: 62.9 us -> 60.7 us  [body(): pl.pallas_call(fused_kernel, out_shape=jax.ShapeDtypeStruct((4, 8, WINDOW...]
where the time goes in v4:
time: 64 us; the launch traced here: 63.8 us
  Pallas kernels  60.7 us (95%)
  local copies, waits for them, and re-layouts  3.11 us (5%)
    pallas_call x1, Pallas kernels, body(): pl.pallas_call(fused_kernel, out_shape=jax.ShapeDtypeStruct((4, 8, WINDOW...  60.7 us
    unnamed x2, local copies, waits for them, and re-layouts  3.11 us

profile of v4, /device:TPU:24, one launch (start us, length us, event | category | flops | bytes accessed | tf_op | source)
XLA Modules:
  0.0 63.8 jit_solution(5909007101202709226)
XLA Ops:
  0.0 1.6 %copy.5.spectra_any = bf16[4,2,33,256]{3,2,1,0:T(8,128)(2,1)} copy(bf16[4,2,33,256]{3,1,2,0:T(2,128)(2,1)} %param.4) | data formatting | bytes 270336 | tf_op args[0]
  1.6 60.7 %shard_map.46 = f32[4,8,729]{2,1,0:T(8,128)} custom-call(bf16[4,2,33,256]{3,2,1,0:T(8,128)(2,1)} %copy.5.spectra_any, s32[2,4]{1,0:T(2,128)} %bitcast.1, f32[9,8,128]{2,1,0:T(8,128)} %constant.4.clone.table_any, bf16[16,2,224,256]{3,2,1,0:T(8,128)(2,1)} %constant.5.clone.tables_any), custom_call_target="tpu_custom_call" | custom-call | tf_op jit(solution)/shard_map/pallas_call | solution.py:587
  62.3 1.5 %copy.7 = f32[4,8,729]{2,1,0:T(8,128)} copy(f32[4,8,729]{2,1,0:T(8,128)} %shard_map.46) | data formatting | bytes 186624

commit v5 on v4

--- a/solution.py
+++ b/solution.py
@@ -167,7 +167,7 @@
 
     for i, part in enumerate(PARTS):
         ready(i)
-        lax.fori_loop(*part, one, 0, unroll=11)
+        lax.fori_loop(*part, one, 0, unroll=part[1] - part[0])
 
     middle()
     energies = []
@@ -206,7 +206,7 @@
             quads[REACH + lag, i] = total
         return carry
 
-    lax.fori_loop(0, LAGS, along_z, 0)
+    lax.fori_loop(0, LAGS, along_z, 0, unroll=3)
 
     half = lax.broadcasted_iota(jnp.int32, (8, 128), 0) < 4
 

time: 64 us -> 63.6 us (level)
  no operation moved by 1% of the time
where the time goes in v5:
time: 63.6 us; the launch traced here: 63.4 us
  Pallas kernels  60.3 us (95%)
  local copies, waits for them, and re-layouts  3.11 us (5%)
    pallas_call x1, Pallas kernels, body(): pl.pallas_call(fused_kernel, out_shape=jax.ShapeDtypeStruct((4, 8, WINDOW...  60.3 us
    unnamed x2, local copies, waits for them, and re-layouts  3.11 us

profile of v5, /device:TPU:24, one launch (start us, length us, event | category | flops | bytes accessed | tf_op | source)
XLA Modules:
  0.0 63.4 jit_solution(7685559936699658583)
XLA Ops:
  0.0 1.6 %copy.5.spectra_any = bf16[4,2,33,256]{3,2,1,0:T(8,128)(2,1)} copy(bf16[4,2,33,256]{3,1,2,0:T(2,128)(2,1)} %param.4) | data formatting | bytes 270336 | tf_op args[0]
  1.6 60.3 %shard_map.46 = f32[4,8,729]{2,1,0:T(8,128)} custom-call(bf16[4,2,33,256]{3,2,1,0:T(8,128)(2,1)} %copy.5.spectra_any, s32[2,4]{1,0:T(2,128)} %bitcast.1, f32[9,8,128]{2,1,0:T(8,128)} %constant.4.clone.table_any, bf16[16,2,224,256]{3,2,1,0:T(8,128)(2,1)} %constant.5.clone.tables_any), custom_call_target="tpu_custom_call" | custom-call | tf_op jit(solution)/shard_map/pallas_call | solution.py:587
  61.9 1.5 %copy.7 = f32[4,8,729]{2,1,0:T(8,128)} copy(f32[4,8,729]{2,1,0:T(8,128)} %shard_map.46) | data formatting | bytes 186624
